TPU v7x, 32 devices: a whole 2x2x4 slice. The times are simulated.
32 devices in a mesh: row: 8 (over z, y), band: 4 (over x, core).
Axes of the slice: x: 2, y: 2, z: 4, core: 2. Of those that a mesh axis runs over, the one named last changes fastest.
Arguments:
- nodes: float32 [8, 3, 512], P('row', None, 'band'), may hold values from -6 to 6
- segments: float32 [8, 6, 3072], P('row', None, 'band'), may hold values from -6 to 6
- circulation: float32 [8, 3072], P('row', 'band'), may hold values from -1 to 1
- upstream: int32 [8, 3], P('row'), may hold values from 0 to 3, as said below
- upstream_mask: int32 [8, 3], P('row'), may hold values from 0 to 1, as said below
Outputs:
- new_nodes: float32 [8, 3, 512], P('row', None, 'band')
- velocity_first: float32 [8, 3, 512], P('row', None, 'band')
Inputs may be any that keep to these rules, and one draw needn't show every extreme that they name: `upstream`: each turbine's used entries come first and name distinct turbines of the previous downwind row of 4 turbines (turbine t lies in downwind row t // 4); unused entries are 0. `upstream_mask`: turbines of the first downwind row use no entries; the last turbine uses all three.
All inputs are finite; a program needn't handle non-finite values.
Results may differ from a plain program's by a relative error of at most 0.00014.
Values sent between devices are 32-bit elements; how exact they have to be, the bound alone decides.
No kernel may reach another device: no remote copies, remote signals or barrier semaphores. Data moves between devices by JAX's collectives and lax.ppermute only.
A program may use at most 64 MiB of HBM per device.

v0:
```python
import functools
import math

import jax
import jax.numpy as jnp
from jax import lax
from jax.experimental import pallas as pl
from jax.experimental.pallas import tpu as pltpu
from jax.sharding import PartitionSpec as P

FIL = 8
CORE_SQUARE = 0.04
AGE_STEP = 0.25
LISTED = 3
TILE = 256
TERMS = 96
SUMS = 32
F32, BF16 = jnp.float32, jnp.bfloat16
VMEM = pl.BlockSpec(memory_space=pltpu.VMEM)
ANY = pl.BlockSpec(memory_space=pl.ANY)
PARAMS = pltpu.CompilerParams(vmem_limit_bytes=32 * 2**20)


def split(value):
    high = value.astype(BF16).astype(F32)
    rest = value - high
    middle = rest.astype(BF16).astype(F32)
    return high, middle, rest - middle


def point_factors(points):
    count = points.shape[1]
    zeros = lambda rows: jnp.zeros((rows, count), F32)
    terms = split(-2.0 * points)
    squared = split(jnp.sum(points * points, axis=0, keepdims=True))
    one = jnp.ones((1, count), F32)
    both = []
    for end in (False, True):
        rows = []
        for term in (0, 1, 2, 0, 1, 2, 0, 1):
            rows += [zeros(3), terms[term], zeros(2)] if end else [terms[term], zeros(5)]
        for _ in range(3):
            rows += [zeros(1), one, zeros(6)] if end else [one, zeros(7)]
        rows += [*squared, zeros(5)]
        both.append(jnp.concatenate(rows, axis=0).T.astype(BF16))
    return jnp.concatenate(both, axis=0)


def segment_factors(block):
    one = jnp.ones((1, block.shape[1]), F32)
    zero = jnp.zeros_like(one)
    start = [block[i : i + 1] for i in range(3)]
    end = [block[i : i + 1] for i in range(3, 6)]
    scale = block[6:7] * (0.5 / math.pi)
    along = [a - b for a, b in zip(start, end)]
    moment = [
        start[1] * end[2] - start[2] * end[1],
        start[2] * end[0] - start[0] * end[2],
        start[0] * end[1] - start[1] * end[0],
    ]
    square = lambda v: v[0] * v[0] + v[1] * v[1] + v[2] * v[2]
    norms = jnp.concatenate(
        [square(start) + CORE_SQUARE, square(end) + CORE_SQUARE] + [zero] * 6, axis=0
    )
    high, middle, low = split(block)
    constant = jnp.concatenate([one] * 3 + [zero] * 5, axis=0)
    distance = jnp.concatenate(
        [high, high, high, middle, middle, middle, low, low, *split(norms), constant], axis=0
    ).astype(BF16)
    weights = jnp.concatenate([scale * v for v in along + moment] + [zero] * 2, axis=0)
    cross = jnp.concatenate([*split(weights), jnp.zeros_like(weights)], axis=0).astype(BF16)
    return distance, cross, square(along) + 2.0 * CORE_SQUARE


def add_tile(factors, distance, cross, length, total):
    points = factors.shape[0] // 2
    squared = jnp.dot(factors, distance, preferred_element_type=F32)
    squared_one, squared_two = squared[:points], squared[points:]
    inverse_one, inverse_two = lax.rsqrt(squared_one), lax.rsqrt(squared_two)
    norms = squared_one * inverse_one + squared_two * inverse_two
    factor = (inverse_one + inverse_two) * pltpu.reciprocal(norms * norms - length, approx=True)
    high = factor.astype(BF16)
    low = (factor - high.astype(F32)).astype(BF16)
    contract = (((1,), (1,)), ((), ()))
    return (
        total
        + lax.dot_general(cross, high, contract, preferred_element_type=F32)
        + lax.dot_general(cross, low, contract, preferred_element_type=F32)
    )


def view_of(buffers, index):
    return tuple(ref.at[index] for ref in buffers)


def add_prepared(factors, view, total):
    distance, cross, length = view
    for tile in range(distance.shape[1] // TILE):
        at = pl.ds(tile * TILE, TILE)
        total = add_tile(factors, distance[:, at], cross[:, at], length[:, at], total)
    return total


def add_part(factors, block, view, total):
    for ref, value in zip(view, segment_factors(block)):
        ref[...] = value
    return add_prepared(factors, view, total)


def for_count(count, most, branch, total):
    run = branch(0)
    for n in range(1, most + 1):
        run = functools.partial(
            lambda n, low, high, t: lax.cond(count < n, low, high, t), n, run, branch(n)
        )
    return run(total)


def used_wakes(plan):
    return jnp.sum(plan[1:2, :])


def slot_of(plan, wake, group):
    listed = jnp.sum(plan[0:1, wake : wake + 1])
    return lax.rem(listed, group) ^ lax.rem(lax.axis_index("row"), group)


def velocity(where_at, total):
    sums = total[0:8] + total[8:16] + total[16:24]
    x, y, z = where_at[0:1], where_at[1:2], where_at[2:3]
    dx, dy, dz = sums[0:1], sums[1:2], sums[2:3]
    return jnp.concatenate(
        [
            y * dz - z * dy + sums[3:4] + 1.0,
            z * dx - x * dz + sums[4:5],
            x * dy - y * dx + sums[5:6],
        ],
        axis=0,
    )


def pack_kernel(nodes, segments, circulation, packed, semaphores):
    count = nodes.shape[2]
    copies = [
        (circulation, packed.at[6:7]),
        *[(segments.at[i], packed.at[i : i + 1]) for i in range(6)],
        *[(nodes.at[i], packed.at[7:8, i * count : (i + 1) * count]) for i in range(3)],
    ]
    packed[7:8] = jnp.zeros((1, packed.shape[1]), F32)
    started = [
        pltpu.make_async_copy(source, target, semaphores.at[i])
        for i, (source, target) in enumerate(copies)
    ]
    for copy in started:
        copy.start()
    for copy in started:
        copy.wait()


def own_kernel(
    count, upstream, mask, own, behind, extended_ref, factors_ref, plan, distance, cross, length, total_ref
):
    plan[0:1, :] = upstream[...]
    plan[1:2, :] = mask[...]
    node_block = lambda block: jnp.concatenate(
        [block[7:8, i * count : (i + 1) * count] for i in range(3)], axis=0
    )
    points = node_block(own[0])
    root = points[:, :FIL]
    at_start = lax.axis_index("band") == 0
    halo = jnp.where(
        at_start, jnp.concatenate([root, root], axis=1), node_block(behind[0])[:, -2 * FIL :]
    )
    extended = jnp.concatenate([halo, points], axis=1)
    extended_ref[...] = extended
    factors = point_factors(extended)
    factors_ref[...] = factors
    total = jnp.zeros(total_ref.shape, F32)
    for part, block in enumerate((own, behind)):
        total = add_part(factors, block[0], view_of((distance, cross, length), part), total)
    total_ref[...] = total


def near_kernel(group, parts, plan, near, factors_ref, before, distance, cross, length, total_ref):
    low = group // 2
    used = used_wakes(plan)
    factors = factors_ref[...]
    total = before[...]
    for wake in range(LISTED):
        slot = slot_of(plan, wake, group)
        add = functools.partial(
            lambda at, view, total: add_part(factors, near[at], view, total),
            slot // low,
            view_of((distance, cross, length), wake * parts),
        )
        here = (wake < used) & (lax.rem(slot, low) == 0)
        total = lax.cond(here, add, lambda total: total, total)
    total_ref[...] = total


def far_kernel(group, parts, plan, far, own, factors_ref, before, *refs):
    low = group // 2
    tops = group // low
    listed, wake_own, total_ref = refs[6:9], refs[9:12], refs[12]
    factors = factors_ref[...]
    used = used_wakes(plan)
    most = LISTED * parts
    count = 0
    sources, targets = [0] * most, [0] * most
    for wake in range(LISTED):
        slot = slot_of(plan, wake, group)
        for part in range(parts):
            wanted = wake < used if part else (wake < used) & (lax.rem(slot, low) != 0)
            source = (lax.rem(slot, low) * parts + part) * tops + slot // low
            for item in range(wake * parts + part + 1):
                taken = wanted & (count == item)
                sources[item] = jnp.where(taken, source, sources[item])
                targets[item] = jnp.where(taken, wake * parts + part, targets[item])
            count = count + wanted.astype(jnp.int32)

    def branch(items):
        def run(total):
            total = add_part(factors, own[0], view_of(wake_own, 2), total)
            for item in range(items):
                view = view_of(listed, targets[item])
                total = add_part(factors, far[sources[item]], view, total)
            return total

        return run

    total_ref[...] = for_count(count, most, branch, before[...])


def last_kernel(group, parts, plan, blocks, extended_ref, factors_ref, before, *refs):
    own, earlier = refs[:3], refs[3:6]
    updated_ref, first_ref = refs[6:8]
    newest, newest_own = refs[8:11], refs[11:14]
    results, semaphores = refs[14:]
    low = group // 2
    tops = group // low
    factors = factors_ref[...]
    used = used_wakes(plan)
    slots = [slot_of(plan, wake, group) for wake in range(LISTED)]
    own_at = blocks.shape[0] - 2 + lax.rem(lax.axis_index("band"), 2)

    def first_branch(wakes):
        def run(total):
            total = add_part(factors, blocks[own_at], view_of(newest_own, 0), total)
            for wake in range(wakes):
                slot = slots[wake]
                for part in range(parts):
                    at = (lax.rem(slot, low) * parts + part) * tops + slot // low
                    view = view_of(newest, wake * parts + part)
                    total = add_part(factors, blocks[at], view, total)
            return total

        return run

    extended = extended_ref[...]
    total = for_count(used, LISTED, first_branch, before[...])
    first = velocity(extended, total)
    results[0] = first[:, 2 * FIL :]
    send_first = [
        pltpu.make_async_copy(results.at[0, i : i + 1], first_ref.at[i], semaphores.at[0, i])
        for i in range(3)
    ]
    for copy in send_first:
        copy.start()

    def shifted(field):
        return jnp.concatenate([field[:, :FIL], field[:, :-FIL]], axis=1)

    lane = lax.broadcasted_iota(jnp.int32, extended.shape, 1)
    at_start = lax.axis_index("band") == 0
    kept = (lane < FIL) | (at_start & (lane >= 2 * FIL) & (lane < 3 * FIL))
    pair = first + shifted(first)
    previous = shifted(extended)
    predicted = jnp.where(kept, extended, previous + AGE_STEP * 0.5 * pair)
    moved = point_factors(predicted)

    def second_branch(wakes):
        views = [view_of(own, part) for part in range(own[0].shape[0])] + [view_of(newest_own, 0)]
        for index in range(wakes * parts):
            views += [view_of(earlier, index), view_of(newest, index)]

        def run(total):
            for view in views:
                total = add_prepared(moved, view, total)
            return total

        return run

    total = for_count(used, LISTED, second_branch, jnp.zeros_like(total))
    second = velocity(predicted, total)
    pair = pair + second + shifted(second)
    updated = (
        previous + AGE_STEP * 0.25 * pair - (extended - 2.0 * previous + shifted(previous)) / 6.0
    )
    results[1] = jnp.where(kept, extended, updated)[:, 2 * FIL :]
    send_updated = [
        pltpu.make_async_copy(results.at[1, i : i + 1], updated_ref.at[i], semaphores.at[1, i])
        for i in range(3)
    ]
    for copy in send_updated:
        copy.start()
    for copy in send_first + send_updated:
        copy.wait()


def buffers(wakes, segs):
    shapes = ((TERMS, segs), BF16), ((SUMS, segs), BF16), ((1, segs), F32)
    return [((wakes, *shape), dtype) for shape, dtype in shapes]


def outs(*specs):
    return tuple(jax.ShapeDtypeStruct(shape, dtype) for shape, dtype in specs)


def cost(points, segs):
    pairs = points * segs
    return pl.CostEstimate(flops=500 * pairs, bytes_accessed=400 * segs, transcendentals=3 * pairs)


def local(nodes, segments, circulation, upstream, upstream_mask):
    rows, bands = lax.axis_size("row"), lax.axis_size("band")
    group = min(8, rows // 2)
    seg_count = segments.shape[2]
    count = nodes.shape[2]
    points = count + 2 * FIL
    sums = ((SUMS, points), F32)

    own = pl.pallas_call(
        pack_kernel,
        out_shape=pltpu.VMEM((8, seg_count), F32),
        in_specs=[ANY] * 3,
        out_specs=VMEM,
        scratch_shapes=[pltpu.SemaphoreType.DMA((10,))],
    )(nodes.transpose(1, 0, 2), segments.transpose(1, 0, 2), circulation)[None]

    low, parts = group // 2, bands // 2
    tops = group // low

    def permuted(blocks, target):
        route = [(i * bands + j, target(i, j)) for i in range(rows) for j in range(bands)]
        return lax.ppermute(blocks, ("row", "band"), route)

    def flipped(blocks, row_flip, band_flip):
        return permuted(blocks, lambda i, j: (i ^ row_flip) * bands + (j ^ band_flip))

    behind = permuted(own, lambda i, j: i * bands + (j + 1) % bands)
    near = [
        permuted(own, lambda i, j: ((i ^ flip) + group) % rows * bands + j)
        for flip in range(0, group, low)
    ]
    extended, factors, plan, *wake_own, total = pl.pallas_call(
        functools.partial(own_kernel, count),
        out_shape=outs(
            ((3, points), F32),
            ((2 * points, TERMS), BF16),
            ((2, LISTED), jnp.int32),
            *buffers(3, seg_count),
            sums,
        ),
        in_specs=[VMEM] * 4,
        out_specs=(VMEM,) * 7,
        compiler_params=PARAMS,
        cost_estimate=cost(points, 2 * seg_count),
    )(upstream, upstream_mask, own, behind)

    *near, total = lax.optimization_barrier((*near, total))
    near = jnp.concatenate(near)
    with_own = flipped(jnp.concatenate([near, own]), 0, 2)
    far = [with_own[:tops]] + [
        flipped(near, row_flip, 2 * band_flip) for row_flip in range(1, low) for band_flip in range(parts)
    ]
    *listed, total = pl.pallas_call(
        functools.partial(near_kernel, group, parts),
        out_shape=outs(*buffers(LISTED * parts, seg_count), sums),
        in_specs=[VMEM] * 4,
        out_specs=(VMEM,) * 4,
        compiler_params=PARAMS,
        cost_estimate=cost(points, LISTED * seg_count),
    )(plan, near, factors, total)
    *far, with_own, total = lax.optimization_barrier((*far, with_own, total))
    across = with_own[tops:]
    far = jnp.concatenate([near, *far, own, across])
    last = flipped(far, 0, 1)
    *held, total = pl.pallas_call(
        functools.partial(far_kernel, group, parts),
        out_shape=outs(*buffers(LISTED * parts, seg_count), *buffers(3, seg_count), sums),
        in_specs=[VMEM] * 11,
        out_specs=(VMEM,) * 7,
        input_output_aliases={5 + i: i for i in range(6)},
        compiler_params=PARAMS,
        cost_estimate=cost(points, LISTED * seg_count),
    )(plan, far, across, factors, total, *listed, *wake_own)
    listed, wake_own = held[:3], held[3:]

    out = ((3, 1, count), F32)
    updated, first = pl.pallas_call(
        functools.partial(last_kernel, group, parts),
        out_shape=outs(out, out),
        in_specs=[VMEM] * 11,
        out_specs=(ANY,) * 2,
        scratch_shapes=[
            *[pltpu.VMEM(shape, dtype) for shape, dtype in buffers(LISTED * parts, seg_count)],
            *[pltpu.VMEM(shape, dtype) for shape, dtype in buffers(1, seg_count)],
            pltpu.VMEM((2, 3, count), F32),
            pltpu.SemaphoreType.DMA((2, 3)),
        ],
        compiler_params=PARAMS,
        cost_estimate=cost(points, 4 * bands * seg_count),
    )(plan, last, extended, factors, total, *wake_own, *listed)
    return updated.transpose(1, 0, 2), first.transpose(1, 0, 2)


def solution(mesh):
    placed = (
        P("row", None, "band"),
        P("row", None, "band"),
        P("row", "band"),
        P("row", None),
        P("row", None),
    )
    return jax.shard_map(
        local,
        mesh=mesh,
        in_specs=placed,
        out_specs=(P("row", None, "band"), P("row", None, "band")),
        check_vma=False,
    )
```

profile of v0, /device:TPU:29, one launch (start us, length us, event | category | flops | bytes accessed | tf_op | source)
XLA Modules:
  0.0 24.7 jit_solution(12715526515716001219)
XLA Ops:
  0.6 0.9 %shard_map.68 = f32[8,768]{1,0:T(8,128)S(1)} custom-call(f32[3,1,128]{2,1,0:T(1,128)} %bitcast.12, f32[6,1,768]{2,1,0:T(1,128)} %bitcast.11, f32[1,768]{1,0:T(1,128)} %circulation.1), custom_call_target="tpu_custom_call" | custom-call | tf_op jit(solution)/shard_map/pallas_call | solution.py:332
  1.5 0.0 copy-start
  1.5 0.0 copy-start.1
  1.5 1.8 %collective-permute-start = (f32[1,8,768]{2,1,0:T(8,128)S(1)}, f32[1,8,768]{2,1,0:T(8,128)S(1)}, u32[]{:S(2)}, u32[]{:S(2)}) collective-permute-start(f32[1,8,768]{2,1,0:T(8,128)S(1)} %bitcast.6), channel_id=1, source_target_pairs={{0,1},{1,2},{2,3},{3,0},{4,5},{5,6},{6,7},{7,4},{8,9},{9,10},{10,1... | collective-permute-start | bytes 73736 | tf_op jit(solution)/shard_map/ppermute | solution.py:345
  3.4 0.0 collective-permute-start.2
  3.4 1.3 %collective-permute-start.1 = (f32[1,8,768]{2,1,0:T(8,128)S(1)}, f32[1,8,768]{2,1,0:T(8,128)S(1)}, u32[]{:S(2)}, u32[]{:S(2)}) collective-permute-start(f32[1,8,768]{2,1,0:T(8,128)S(1)} %bitcast.8), channel_id=1, source_target_pairs={{0,16},{1,17},{2,18},{3,19},{4,20},{5,21},{6,22},{7,23},{8,24},{9,... | collective-permute-start | bytes 73736 | tf_op jit(solution)/shard_map/ppermute | solution.py:345
  4.7 0.0 collective-permute-done.behind
  4.7 0.0 copy-done
  4.7 0.0 copy-done.1
  4.7 0.9 %shard_map.69 = (f32[3,144]{1,0:T(4,128)S(1)}, bf16[288,96]{1,0:T(8,128)(2,1)S(1)}, s32[2,3]{1,0:T(2,128)S(1)}, bf16[3,96,768]{2,1,0:T(8,128)(2,1)S(1)}, bf16[3,...) custom-call(s32[1,3]{1,0:T(1,128)S(1)} %copy-done, s32[1,3]{1,0:T(1,128)S(1)} %copy-done.1, ...), custom_call_target="tpu_custom_call" | custom-call | flops 110592000 | bytes 614400 | tf_op jit(solution)/shard_map/pallas_call | solution.py:355
  5.7 2.2 %collective-permute-done.2 = f32[1,8,768]{2,1,0:T(8,128)S(1)} collective-permute-done((f32[1,8,768]{2,1,0:T(8,128)S(1)}, f32[1,8,768]{2,1,0:T(8,128)S(1)}, u32[]{:S(2)}, u32[]{:S(2)}) %collective-permute-start.2) | collective-permute-done | bytes 24608 | tf_op jit(solution)/shard_map/ppermute | solution.py:345
  7.8 0.0 collective-permute-done.1
  7.9 0.3 %collective-permute-start.3 = (f32[3,8,768]{2,1,0:T(8,128)S(1)}, f32[3,8,768]{2,1,0:T(8,128)S(1)}, u32[]{:S(2)}, u32[]{:S(2)}) collective-permute-start(f32[3,8,768]{2,1,0:T(8,128)S(1)} %pad_maximum_fusion), channel_id=1, source_target_pairs={{0,2},{1,3},{2,0},{3,1},{4,6},{5,7},{6,4},{7,5},{8,10},{9,11},{10,... | collective-permute-start | bytes 221192 | tf_op jit(solution)/shard_map/ppermute | solution.py:345
  8.2 1.2 %collective-permute-start.5 = (f32[2,8,768]{2,1,0:T(8,128)S(1)}, f32[2,8,768]{2,1,0:T(8,128)S(1)}, u32[]{:S(2)}, u32[]{:S(2)}) collective-permute-start(f32[2,8,768]{2,1,0:T(8,128)S(1)} %get-tuple-element.60.near), channel_id=1, source_target_pairs={{0,6},{1,7},{2,4},{3,5},{4,2},{5,3},{6,0},{7,1},{8,14},{9,15},{10,... | collective-permute-start | bytes 147464 | tf_op jit(solution)/shard_map/ppermute | solution.py:345
  9.3 1.2 %collective-permute-start.4 = (f32[2,8,768]{2,1,0:T(8,128)S(1)}, f32[2,8,768]{2,1,0:T(8,128)S(1)}, u32[]{:S(2)}, u32[]{:S(2)}) collective-permute-start(f32[2,8,768]{2,1,0:T(8,128)S(1)} %get-tuple-element.60.near), channel_id=1, source_target_pairs={{0,4},{1,5},{2,6},{3,7},{4,0},{5,1},{6,2},{7,3},{8,12},{9,13},{10,... | collective-permute-start | bytes 147464 | tf_op jit(solution)/shard_map/ppermute | solution.py:345
  10.6 1.5 %shard_map.70 = (bf16[6,96,768]{2,1,0:T(8,128)(2,1)S(1)}, bf16[6,32,768]{2,1,0:T(8,128)(2,1)S(1)}, f32[6,1,768]{2,1,0:T(1,128)S(1)}, f32[32,144]{1,0:T(8,128)S(1)}) custom-call(s32[2,3]{1,0:T(2,128)S(1)} %get-tuple-element.30.plan, f32[2,8,768]{2,1,0:T(8,128)S(1)} %get-tuple-element.60.near, bf16[288,96]{1,0:T(8,128)(2,1)S(1)} %get-tuple-element.34.factors_ref, ...), custom_call_target="tpu_custom_call" | custom-call | flops 165888000 | bytes 921600 | tf_op jit(solution)/shard_map/pallas_call | solution.py:376
  12.1 0.0 collective-permute-done.3
  12.1 0.4 %collective-permute-done.5 = f32[2,8,768]{2,1,0:T(8,128)S(1)} collective-permute-done((f32[2,8,768]{2,1,0:T(8,128)S(1)}, f32[2,8,768]{2,1,0:T(8,128)S(1)}, u32[]{:S(2)}, u32[]{:S(2)}) %collective-permute-start.5) | collective-permute-done | bytes 49184 | tf_op jit(solution)/shard_map/ppermute | solution.py:345
  12.5 0.2 collective-permute-done.4
  12.8 2.0 %collective-permute-start.6 = (f32[10,8,768]{2,1,0:T(8,128)S(1)}, f32[10,8,768]{2,1,0:T(8,128)S(1)}, u32[]{:S(2)}, u32[]{:S(2)}) collective-permute-start(f32[10,8,768]{2,1,0:T(8,128)S(1)} %get-tuple-element.59.far), channel_id=1, source_target_pairs={{0,1},{1,0},{2,3},{3,2},{4,5},{5,4},{6,7},{7,6},{8,9},{9,8},{10,11... | collective-permute-start | bytes 737288 | tf_op jit(solution)/shard_map/ppermute | solution.py:345
  14.8 1.9 %shard_map.71 = (bf16[6,96,768]{2,1,0:T(8,128)(2,1)S(1)}, bf16[6,32,768]{2,1,0:T(8,128)(2,1)S(1)}, f32[6,1,768]{2,1,0:T(1,128)S(1)}, bf16[3,96,768]{2,1,0:T(8,12...) custom-call(s32[2,3]{1,0:T(2,128)S(1)} %get-tuple-element.30.plan, ...), custom_call_target="tpu_custom_call", output_to_operand_aliasing={{0}: (5, {}), {1}: (6, {}), {2}: (7, {}), {3}: (8, {}), {4}... | custom-call | flops 165888000 | bytes 921600 | tf_op jit(solution)/shard_map/pallas_call | solution.py:388
  16.7 0.0 collective-permute-done.6.blocks
  16.7 7.8 %shard_map.72 = (f32[3,1,128]{2,1,0:T(1,128)}, f32[3,1,128]{2,1,0:T(1,128)}) custom-call(s32[2,3]{1,0:T(2,128)S(1)} %get-tuple-element.30.plan, f32[10,8,768]{2,1,0:T(8,128)S(1)} %collective-permute-done.6.blocks, f32[3,144]{1,0:T(4,128)S(1)} %get-tuple-element.41.extended_ref, bf16[288,96]{1,0:T(8,128)(2,1)S(1)} %get-tuple-element.34.factors_ref, ...), custom_call_target="tpu_custom_call" | custom-call | flops 884736000 | bytes 4915200 | tf_op jit(solution)/shard_map/pallas_call | solution.py:400
  (9 shorter events, 0.0 us)
Async XLA Ops:
  1.5 3.2 %copy-start = (s32[1,3]{1,0:T(1,128)S(1)}, s32[1,3]{1,0:T(1,128)}, u32[]{:S(2)}) copy-start(s32[1,3]{1,0:T(1,128)} %upstream.1) | copy-start | bytes 40
  1.5 3.2 %copy-start.1 = (s32[1,3]{1,0:T(1,128)S(1)}, s32[1,3]{1,0:T(1,128)}, u32[]{:S(2)}) copy-start(s32[1,3]{1,0:T(1,128)} %mask.1) | copy-start | bytes 40
  1.5 3.2 %collective-permute-start = (f32[1,8,768]{2,1,0:T(8,128)S(1)}, f32[1,8,768]{2,1,0:T(8,128)S(1)}, u32[]{:S(2)}, u32[]{:S(2)}) collective-permute-start(f32[1,8,768]{2,1,0:T(8,128)S(1)} %bitcast.6), channel_id=1, source_target_pairs={{0,1},{1,2},{2,3},{3,0},{4,5},{5,6},{6,7},{7,4},{8,9},{9,10},{10,1... | collective-permute-start | bytes 73736 | tf_op jit(solution)/shard_map/ppermute | solution.py:345
  3.4 4.5 %collective-permute-start.2 = (f32[1,8,768]{2,1,0:T(8,128)S(1)}, f32[1,8,768]{2,1,0:T(8,128)S(1)}, u32[]{:S(2)}, u32[]{:S(2)}) collective-permute-start(f32[1,8,768]{2,1,0:T(8,128)S(1)} %bitcast.7), channel_id=1, source_target_pairs={{0,24},{1,25},{2,26},{3,27},{4,28},{5,29},{6,30},{7,31},{8,16},{9,... | collective-permute-start | bytes 73736 | tf_op jit(solution)/shard_map/ppermute | solution.py:345
  3.4 4.5 %collective-permute-start.1 = (f32[1,8,768]{2,1,0:T(8,128)S(1)}, f32[1,8,768]{2,1,0:T(8,128)S(1)}, u32[]{:S(2)}, u32[]{:S(2)}) collective-permute-start(f32[1,8,768]{2,1,0:T(8,128)S(1)} %bitcast.8), channel_id=1, source_target_pairs={{0,16},{1,17},{2,18},{3,19},{4,20},{5,21},{6,22},{7,23},{8,24},{9,... | collective-permute-start | bytes 73736 | tf_op jit(solution)/shard_map/ppermute | solution.py:345
  7.9 4.2 %collective-permute-start.3 = (f32[3,8,768]{2,1,0:T(8,128)S(1)}, f32[3,8,768]{2,1,0:T(8,128)S(1)}, u32[]{:S(2)}, u32[]{:S(2)}) collective-permute-start(f32[3,8,768]{2,1,0:T(8,128)S(1)} %pad_maximum_fusion), channel_id=1, source_target_pairs={{0,2},{1,3},{2,0},{3,1},{4,6},{5,7},{6,4},{7,5},{8,10},{9,11},{10,... | collective-permute-start | bytes 221192 | tf_op jit(solution)/shard_map/ppermute | solution.py:345
  8.2 4.3 %collective-permute-start.5 = (f32[2,8,768]{2,1,0:T(8,128)S(1)}, f32[2,8,768]{2,1,0:T(8,128)S(1)}, u32[]{:S(2)}, u32[]{:S(2)}) collective-permute-start(f32[2,8,768]{2,1,0:T(8,128)S(1)} %get-tuple-element.60.near), channel_id=1, source_target_pairs={{0,6},{1,7},{2,4},{3,5},{4,2},{5,3},{6,0},{7,1},{8,14},{9,15},{10,... | collective-permute-start | bytes 147464 | tf_op jit(solution)/shard_map/ppermute | solution.py:345
  9.3 3.4 %collective-permute-start.4 = (f32[2,8,768]{2,1,0:T(8,128)S(1)}, f32[2,8,768]{2,1,0:T(8,128)S(1)}, u32[]{:S(2)}, u32[]{:S(2)}) collective-permute-start(f32[2,8,768]{2,1,0:T(8,128)S(1)} %get-tuple-element.60.near), channel_id=1, source_target_pairs={{0,4},{1,5},{2,6},{3,7},{4,0},{5,1},{6,2},{7,3},{8,12},{9,13},{10,... | collective-permute-start | bytes 147464 | tf_op jit(solution)/shard_map/ppermute | solution.py:345
  12.8 3.9 %collective-permute-start.6 = (f32[10,8,768]{2,1,0:T(8,128)S(1)}, f32[10,8,768]{2,1,0:T(8,128)S(1)}, u32[]{:S(2)}, u32[]{:S(2)}) collective-permute-start(f32[10,8,768]{2,1,0:T(8,128)S(1)} %get-tuple-element.59.far), channel_id=1, source_target_pairs={{0,1},{1,0},{2,3},{3,2},{4,5},{5,4},{6,7},{7,6},{8,9},{9,8},{10,11... | collective-permute-start | bytes 737288 | tf_op jit(solution)/shard_map/ppermute | solution.py:345
where the time goes:
time: 25.1 us; the launch traced here: 24.7 us
  Pallas kernels  13 us (52%)
  starting transfers between devices  7.9 us (31%)
  waiting for transfers between devices  2.85 us (11%)
  between operations  0.92 us (4%)
    ppermute x7, starting transfers between devices, permuted(): return lax.ppermute(blocks, ('row', 'band'), route)  7.9 us
    pallas_call x1, Pallas kernels, local(): pl.pallas_call(functools.partial(last_kernel, group, parts), out_shape=ou...  7.83 us
    ppermute x7, waiting for transfers between devices, permuted(): return lax.ppermute(blocks, ('row', 'band'), route)  2.85 us
    pallas_call x1, Pallas kernels, local(): pl.pallas_call(functools.partial(far_kernel, group, parts), out_shape=out...  1.9 us
    pallas_call x1, Pallas kernels, local(): pl.pallas_call(functools.partial(near_kernel, group, parts), out_shape=ou...  1.48 us
    pallas_call x1, Pallas kernels, local(): pl.pallas_call(functools.partial(own_kernel, count), out_shape=outs(((3,...  0.93 us
    pallas_call x1, Pallas kernels, local(): pl.pallas_call(pack_kernel, out_shape=pltpu.VMEM((8, seg_count), F32), in...  0.88 us
  transfers between devices with their start and end apart: 7, of which 3 were waited for; matrix products, arithmetic and copies ran while one was open for 0% of the time, Pallas kernels for 17%

commit v1 on v0

--- a/solution.py
+++ b/solution.py
@@ -32,18 +32,15 @@
     count = points.shape[1]
     zeros = lambda rows: jnp.zeros((rows, count), F32)
     terms = split(-2.0 * points)
-    squared = split(jnp.sum(points * points, axis=0, keepdims=True))
     one = jnp.ones((1, count), F32)
-    both = []
-    for end in (False, True):
-        rows = []
-        for term in (0, 1, 2, 0, 1, 2, 0, 1):
-            rows += [zeros(3), terms[term], zeros(2)] if end else [terms[term], zeros(5)]
-        for _ in range(3):
-            rows += [zeros(1), one, zeros(6)] if end else [one, zeros(7)]
-        rows += [*squared, zeros(5)]
-        both.append(jnp.concatenate(rows, axis=0).T.astype(BF16))
-    return jnp.concatenate(both, axis=0)
+    rows = []
+    for term in (0, 1, 2, 0, 1, 2, 0, 1):
+        rows += [terms[term], zeros(5)]
+    rows += [one, zeros(7)] * 3
+    rows += [*split(jnp.sum(points * points, axis=0, keepdims=True)), zeros(128 - TERMS + 5)]
+    first = jnp.concatenate(rows, axis=0).T
+    both = jnp.concatenate([first, pltpu.roll(first, 3, 1)], axis=0)
+    return both[:, :TERMS].astype(BF16)
 
 
 def segment_factors(block):
@@ -60,10 +57,10 @@
     ]
     square = lambda v: v[0] * v[0] + v[1] * v[1] + v[2] * v[2]
     norms = jnp.concatenate(
-        [square(start) + CORE_SQUARE, square(end) + CORE_SQUARE] + [zero] * 6, axis=0
+        [square(start) + CORE_SQUARE, zero, zero, square(end) + CORE_SQUARE] + [zero] * 4, axis=0
     )
     high, middle, low = split(block)
-    constant = jnp.concatenate([one] * 3 + [zero] * 5, axis=0)
+    constant = jnp.concatenate([one] * 6 + [zero] * 2, axis=0)
     distance = jnp.concatenate(
         [high, high, high, middle, middle, middle, low, low, *split(norms), constant], axis=0
     ).astype(BF16)
@@ -143,7 +140,7 @@
     count = nodes.shape[2]
     copies = [
         (circulation, packed.at[6:7]),
-        *[(segments.at[i], packed.at[i : i + 1]) for i in range(6)],
+        (segments.at[:, 0], packed.at[0:6]),
         *[(nodes.at[i], packed.at[7:8, i * count : (i + 1) * count]) for i in range(3)],
     ]
     packed[7:8] = jnp.zeros((1, packed.shape[1]), F32)
@@ -181,54 +178,46 @@
     total_ref[...] = total
 
 
-def near_kernel(group, parts, plan, near, factors_ref, before, distance, cross, length, total_ref):
+def parts_kernel(group, parts, wanted, most, plan, blocks, factors_ref, before, *refs):
     low = group // 2
-    used = used_wakes(plan)
-    factors = factors_ref[...]
-    total = before[...]
-    for wake in range(LISTED):
-        slot = slot_of(plan, wake, group)
-        add = functools.partial(
-            lambda at, view, total: add_part(factors, near[at], view, total),
-            slot // low,
-            view_of((distance, cross, length), wake * parts),
-        )
-        here = (wake < used) & (lax.rem(slot, low) == 0)
-        total = lax.cond(here, add, lambda total: total, total)
-    total_ref[...] = total
-
-
-def far_kernel(group, parts, plan, far, own, factors_ref, before, *refs):
-    low = group // 2
-    tops = group // low
-    listed, wake_own, total_ref = refs[6:9], refs[9:12], refs[12]
+    total_ref = refs[-1]
+    views = refs[len(refs) // 2 : -1]
+    listed, wake_own = views[:3], views[3:]
     factors = factors_ref[...]
     used = used_wakes(plan)
-    most = LISTED * parts
     count = 0
     sources, targets = [0] * most, [0] * most
     for wake in range(LISTED):
         slot = slot_of(plan, wake, group)
+        same = lax.rem(slot, low) == 0
         for part in range(parts):
-            wanted = wake < used if part else (wake < used) & (lax.rem(slot, low) != 0)
-            source = (lax.rem(slot, low) * parts + part) * tops + slot // low
-            for item in range(wake * parts + part + 1):
-                taken = wanted & (count == item)
-                sources[item] = jnp.where(taken, source, sources[item])
-                targets[item] = jnp.where(taken, wake * parts + part, targets[item])
-            count = count + wanted.astype(jnp.int32)
+            chosen, source = wanted(same, part, lax.rem(slot, low), slot // low)
+            if chosen is None:
+                continue
+            taken = chosen & (wake < used)
+            for item in range(most):
+                here = taken & (count == item)
+                sources[item] = jnp.where(here, source, sources[item])
+                targets[item] = jnp.where(here, wake * parts + part, targets[item])
+            count = count + taken.astype(jnp.int32)
 
     def branch(items):
         def run(total):
-            total = add_part(factors, own[0], view_of(wake_own, 2), total)
+            if wake_own:
+                total = add_part(factors, blocks[blocks.shape[0] - 1], view_of(wake_own, 2), total)
             for item in range(items):
                 view = view_of(listed, targets[item])
-                total = add_part(factors, far[sources[item]], view, total)
+                total = add_part(factors, blocks[sources[item]], view, total)
             return total
 
         return run
 
     total_ref[...] = for_count(count, most, branch, before[...])
+
+
+def first_parts_kernel(group, parts, most, plan, blocks, factors_ref, before, *refs):
+    wanted = lambda same, part, bits, top: (None, None) if part else (same, top)
+    parts_kernel(group, parts, wanted, most, plan, blocks, factors_ref, before, *[None] * 3, *refs)
 
 
 def last_kernel(group, parts, plan, blocks, extended_ref, factors_ref, before, *refs):
@@ -334,7 +323,7 @@
         out_shape=pltpu.VMEM((8, seg_count), F32),
         in_specs=[ANY] * 3,
         out_specs=VMEM,
-        scratch_shapes=[pltpu.SemaphoreType.DMA((10,))],
+        scratch_shapes=[pltpu.SemaphoreType.DMA((5,))],
     )(nodes.transpose(1, 0, 2), segments.transpose(1, 0, 2), circulation)[None]
 
     low, parts = group // 2, bands // 2
@@ -367,34 +356,51 @@
         cost_estimate=cost(points, 2 * seg_count),
     )(upstream, upstream_mask, own, behind)
 
+    def add_parts(wanted, most, blocks, total, held):
+        *held, total = pl.pallas_call(
+            functools.partial(parts_kernel, group, parts, wanted, most),
+            out_shape=outs(*[(array.shape, array.dtype) for array in held], sums),
+            in_specs=[VMEM] * (4 + len(held)),
+            out_specs=(VMEM,) * (1 + len(held)),
+            input_output_aliases={4 + i: i for i in range(len(held))},
+            compiler_params=PARAMS,
+            cost_estimate=cost(points, LISTED * seg_count),
+        )(plan, blocks, factors, total, *held)
+        return held, total
+
     *near, total = lax.optimization_barrier((*near, total))
     near = jnp.concatenate(near)
     with_own = flipped(jnp.concatenate([near, own]), 0, 2)
-    far = [with_own[:tops]] + [
+    far = [
         flipped(near, row_flip, 2 * band_flip) for row_flip in range(1, low) for band_flip in range(parts)
     ]
+    some = min(LISTED, tops)
     *listed, total = pl.pallas_call(
-        functools.partial(near_kernel, group, parts),
+        functools.partial(first_parts_kernel, group, parts, some),
         out_shape=outs(*buffers(LISTED * parts, seg_count), sums),
         in_specs=[VMEM] * 4,
         out_specs=(VMEM,) * 4,
         compiler_params=PARAMS,
         cost_estimate=cost(points, LISTED * seg_count),
     )(plan, near, factors, total)
-    *far, with_own, total = lax.optimization_barrier((*far, with_own, total))
-    across = with_own[tops:]
-    far = jnp.concatenate([near, *far, own, across])
+
+    def brought_across(same, part, bits, top):
+        return (same, (part - 1) * tops + top) if part else (None, None)
+
+    def brought_along(same, part, bits, top):
+        return ~same, (bits * parts + part) * tops + top
+
+    with_own, total = lax.optimization_barrier((with_own, total))
+    held, total = add_parts(
+        brought_across, some * (parts - 1), with_own, total, [*listed, *wake_own]
+    )
+    listed, wake_own = held[:3], held[3:]
+    *far, total = lax.optimization_barrier((*far, total))
+    far = jnp.concatenate([near, with_own[:tops], *far, own, with_own[tops:]])
     last = flipped(far, 0, 1)
-    *held, total = pl.pallas_call(
-        functools.partial(far_kernel, group, parts),
-        out_shape=outs(*buffers(LISTED * parts, seg_count), *buffers(3, seg_count), sums),
-        in_specs=[VMEM] * 11,
-        out_specs=(VMEM,) * 7,
-        input_output_aliases={5 + i: i for i in range(6)},
-        compiler_params=PARAMS,
-        cost_estimate=cost(points, LISTED * seg_count),
-    )(plan, far, across, factors, total, *listed, *wake_own)
-    listed, wake_own = held[:3], held[3:]
+    listed, total = add_parts(
+        brought_along, min(LISTED, group - tops) * parts, far, total, listed
+    )
 
     out = ((3, 1, count), F32)
     updated, first = pl.pallas_call(

time: 25.1 us -> 25 us (level); the launches traced: 24.7 us -> 25.1 us
  starting transfers between devices: 7.9 us -> 9.64 us
  waiting for transfers between devices: 2.85 us -> 1.62 us
    ppermute x7, starting transfers between devices: 7.9 us -> 9.64 us  [permuted(): return lax.ppermute(blocks, ('row', 'band'), route)]
    ppermute x7, waiting for transfers between devices: 2.85 us -> 1.62 us  [permuted(): return lax.ppermute(blocks, ('row', 'band'), route)]
    pallas_call x2 -> x3, Pallas kernels: 3.37 us -> 3.19 us  [the longest x2 2.51 us: add_parts(): pl.pallas_call(functools.partial(parts_kernel, group, parts, wanted, most...]
where the time goes in v1:
time: 25 us; the launch traced here: 25.1 us
  Pallas kernels  12.8 us (51%)
  starting transfers between devices  9.64 us (39%)
  waiting for transfers between devices  1.62 us (6%)
  between operations  0.9 us (4%)
    ppermute x7, starting transfers between devices, permuted(): return lax.ppermute(blocks, ('row', 'band'), route)  9.64 us
    pallas_call x1, Pallas kernels, local(): pl.pallas_call(functools.partial(last_kernel, group, parts), out_shape=ou...  7.85 us
    pallas_call x2, Pallas kernels, add_parts(): pl.pallas_call(functools.partial(parts_kernel, group, parts, wanted, most...  2.51 us
    ppermute x7, waiting for transfers between devices, permuted(): return lax.ppermute(blocks, ('row', 'band'), route)  1.62 us
    pallas_call x1, Pallas kernels, local(): pl.pallas_call(functools.partial(own_kernel, count), out_shape=outs(((3,...  1 us
    pallas_call x1, Pallas kernels, local(): pl.pallas_call(pack_kernel, out_shape=pltpu.VMEM((8, seg_count), F32), in...  0.79 us
    pallas_call x1, Pallas kernels, local(): pl.pallas_call(functools.partial(first_parts_kernel, group, parts, some),...  0.68 us
  transfers between devices with their start and end apart: 7, of which 3 were waited for; matrix products, arithmetic and copies ran while one was open for 0% of the time, Pallas kernels for 17%

profile of v1, /device:TPU:29, one launch (start us, length us, event | category | flops | bytes accessed | tf_op | source)
XLA Modules:
  0.0 25.1 jit_solution(1715088674074110153)
XLA Ops:
  0.6 0.8 %shard_map.68 = f32[8,768]{1,0:T(8,128)S(1)} custom-call(f32[3,1,128]{2,1,0:T(1,128)} %bitcast.12, f32[6,1,768]{2,1,0:T(1,128)} %bitcast.11, f32[1,768]{1,0:T(1,128)} %circulation.1), custom_call_target="tpu_custom_call" | custom-call | tf_op jit(solution)/shard_map/pallas_call | solution.py:321
  1.4 0.0 copy-start
  1.4 0.0 copy-start.1
  1.5 1.8 %collective-permute-start = (f32[1,8,768]{2,1,0:T(8,128)S(1)}, f32[1,8,768]{2,1,0:T(8,128)S(1)}, u32[]{:S(2)}, u32[]{:S(2)}) collective-permute-start(f32[1,8,768]{2,1,0:T(8,128)S(1)} %bitcast.6), channel_id=1, source_target_pairs={{0,1},{1,2},{2,3},{3,0},{4,5},{5,6},{6,7},{7,4},{8,9},{9,10},{10,1... | collective-permute-start | bytes 73736 | tf_op jit(solution)/shard_map/ppermute | solution.py:334
  3.3 0.1 collective-permute-start.1
  3.3 2.2 %collective-permute-start.2 = (f32[1,8,768]{2,1,0:T(8,128)S(1)}, f32[1,8,768]{2,1,0:T(8,128)S(1)}, u32[]{:S(2)}, u32[]{:S(2)}) collective-permute-start(f32[1,8,768]{2,1,0:T(8,128)S(1)} %bitcast.8), channel_id=1, source_target_pairs={{0,24},{1,25},{2,26},{3,27},{4,28},{5,29},{6,30},{7,31},{8,16},{9,... | collective-permute-start | bytes 73736 | tf_op jit(solution)/shard_map/ppermute | solution.py:334
  5.5 0.0 collective-permute-done.behind
  5.5 0.0 copy-done
  5.5 0.0 copy-done.1
  5.5 1.0 %shard_map.69 = (f32[3,144]{1,0:T(4,128)S(1)}, bf16[288,96]{1,0:T(8,128)(2,1)S(1)}, s32[2,3]{1,0:T(2,128)S(1)}, bf16[3,96,768]{2,1,0:T(8,128)(2,1)S(1)}, bf16[3,...) custom-call(s32[1,3]{1,0:T(1,128)S(1)} %copy-done, s32[1,3]{1,0:T(1,128)S(1)} %copy-done.1, ...), custom_call_target="tpu_custom_call" | custom-call | flops 110592000 | bytes 614400 | tf_op jit(solution)/shard_map/pallas_call | solution.py:344
  6.5 1.0 %collective-permute-done.1 = f32[1,8,768]{2,1,0:T(8,128)S(1)} collective-permute-done((f32[1,8,768]{2,1,0:T(8,128)S(1)}, f32[1,8,768]{2,1,0:T(8,128)S(1)}, u32[]{:S(2)}, u32[]{:S(2)}) %collective-permute-start.1) | collective-permute-done | bytes 24608 | tf_op jit(solution)/shard_map/ppermute | solution.py:334
  7.5 0.4 %collective-permute-done.2 = f32[1,8,768]{2,1,0:T(8,128)S(1)} collective-permute-done((f32[1,8,768]{2,1,0:T(8,128)S(1)}, f32[1,8,768]{2,1,0:T(8,128)S(1)}, u32[]{:S(2)}, u32[]{:S(2)}) %collective-permute-start.2) | collective-permute-done | bytes 24608 | tf_op jit(solution)/shard_map/ppermute | solution.py:334
  7.9 0.2 collective-permute-start.3
  8.1 0.2 collective-permute-start.4
  8.4 2.3 %collective-permute-start.5 = (f32[2,8,768]{2,1,0:T(8,128)S(1)}, f32[2,8,768]{2,1,0:T(8,128)S(1)}, u32[]{:S(2)}, u32[]{:S(2)}) collective-permute-start(f32[2,8,768]{2,1,0:T(8,128)S(1)} %get-tuple-element.66.blocks), channel_id=1, source_target_pairs={{0,6},{1,7},{2,4},{3,5},{4,2},{5,3},{6,0},{7,1},{8,14},{9,15},{10,... | collective-permute-start | bytes 147464 | tf_op jit(solution)/shard_map/ppermute | solution.py:334
  10.6 0.7 %shard_map.70 = (bf16[6,96,768]{2,1,0:T(8,128)(2,1)S(1)}, bf16[6,32,768]{2,1,0:T(8,128)(2,1)S(1)}, f32[6,1,768]{2,1,0:T(1,128)S(1)}, f32[32,144]{1,0:T(8,128)S(1)}) custom-call(s32[2,3]{1,0:T(2,128)S(1)} %get-tuple-element.34.plan, f32[2,8,768]{2,1,0:T(8,128)S(1)} %get-tuple-element.66.blocks, bf16[288,96]{1,0:T(8,128)(2,1)S(1)} %get-tuple-element.38.factors_ref, ...), custom_call_target="tpu_custom_call" | custom-call | flops 165888000 | bytes 921600 | tf_op jit(solution)/shard_map/pallas_call | solution.py:378
  11.3 0.0 collective-permute-done.3.blocks
  11.4 1.0 %shard_map.71 = (bf16[6,96,768]{2,1,0:T(8,128)(2,1)S(1)}, bf16[6,32,768]{2,1,0:T(8,128)(2,1)S(1)}, f32[6,1,768]{2,1,0:T(1,128)S(1)}, bf16[3,96,768]{2,1,0:T(8,12...) custom-call(s32[2,3]{1,0:T(2,128)S(1)} %get-tuple-element.34.plan, ...), custom_call_target="tpu_custom_call", output_to_operand_aliasing={{0}: (4, {}), {1}: (5, {}), {2}: (6, {}), {3}: (7, {}), {4}... | custom-call | flops 165888000 | bytes 921600 | tf_op jit(solution)/shard_map/pallas_call | solution.py:360
  12.3 0.0 collective-permute-done.4
  12.4 0.2 collective-permute-done.5
  12.6 2.9 %collective-permute-start.6 = (f32[10,8,768]{2,1,0:T(8,128)S(1)}, f32[10,8,768]{2,1,0:T(8,128)S(1)}, u32[]{:S(2)}, u32[]{:S(2)}) collective-permute-start(f32[10,8,768]{2,1,0:T(8,128)S(1)} %slice_dynamic-update-slice_fusion.1.blocks), channel_id=1, source_target_pairs={{0,1},{1,0},{2,3},{3,2},{4,5},{5,4},{6,7},{7,6},{8,9},{9,8},{10,11... | collective-permute-start | bytes 737288 | tf_op jit(solution)/shard_map/ppermute | solution.py:334
  15.4 1.5 %shard_map.72 = (bf16[6,96,768]{2,1,0:T(8,128)(2,1)S(1)}, bf16[6,32,768]{2,1,0:T(8,128)(2,1)S(1)}, f32[6,1,768]{2,1,0:T(1,128)S(1)}, f32[32,144]{1,0:T(8,128)S(1)}) custom-call(s32[2,3]{1,0:T(2,128)S(1)} %get-tuple-element.34.plan, ...), custom_call_target="tpu_custom_call", output_to_operand_aliasing={{0}: (4, {}), {1}: (5, {}), {2}: (6, {})} | custom-call | flops 165888000 | bytes 921600 | tf_op jit(solution)/shard_map/pallas_call | solution.py:360
  17.0 0.0 collective-permute-done.6.blocks
  17.0 7.8 %shard_map.73 = (f32[3,1,128]{2,1,0:T(1,128)}, f32[3,1,128]{2,1,0:T(1,128)}) custom-call(s32[2,3]{1,0:T(2,128)S(1)} %get-tuple-element.34.plan, f32[10,8,768]{2,1,0:T(8,128)S(1)} %collective-permute-done.6.blocks, f32[3,144]{1,0:T(4,128)S(1)} %get-tuple-element.52.extended_ref, bf16[288,96]{1,0:T(8,128)(2,1)S(1)} %get-tuple-element.38.factors_ref, ...), custom_call_target="tpu_custom_call" | custom-call | flops 884736000 | bytes 4915200 | tf_op jit(solution)/shard_map/pallas_call | solution.py:406
  (8 shorter events, 0.0 us)
Async XLA Ops:
  1.4 4.1 %copy-start = (s32[1,3]{1,0:T(1,128)S(1)}, s32[1,3]{1,0:T(1,128)}, u32[]{:S(2)}) copy-start(s32[1,3]{1,0:T(1,128)} %upstream.1) | copy-start | bytes 40
  1.4 4.1 %copy-start.1 = (s32[1,3]{1,0:T(1,128)S(1)}, s32[1,3]{1,0:T(1,128)}, u32[]{:S(2)}) copy-start(s32[1,3]{1,0:T(1,128)} %mask.1) | copy-start | bytes 40
  1.5 4.1 %collective-permute-start = (f32[1,8,768]{2,1,0:T(8,128)S(1)}, f32[1,8,768]{2,1,0:T(8,128)S(1)}, u32[]{:S(2)}, u32[]{:S(2)}) collective-permute-start(f32[1,8,768]{2,1,0:T(8,128)S(1)} %bitcast.6), channel_id=1, source_target_pairs={{0,1},{1,2},{2,3},{3,0},{4,5},{5,6},{6,7},{7,4},{8,9},{9,10},{10,1... | collective-permute-start | bytes 73736 | tf_op jit(solution)/shard_map/ppermute | solution.py:334
  3.3 4.3 %collective-permute-start.1 = (f32[1,8,768]{2,1,0:T(8,128)S(1)}, f32[1,8,768]{2,1,0:T(8,128)S(1)}, u32[]{:S(2)}, u32[]{:S(2)}) collective-permute-start(f32[1,8,768]{2,1,0:T(8,128)S(1)} %bitcast.7), channel_id=1, source_target_pairs={{0,16},{1,17},{2,18},{3,19},{4,20},{5,21},{6,22},{7,23},{8,24},{9,... | collective-permute-start | bytes 73736 | tf_op jit(solution)/shard_map/ppermute | solution.py:334
  3.3 4.6 %collective-permute-start.2 = (f32[1,8,768]{2,1,0:T(8,128)S(1)}, f32[1,8,768]{2,1,0:T(8,128)S(1)}, u32[]{:S(2)}, u32[]{:S(2)}) collective-permute-start(f32[1,8,768]{2,1,0:T(8,128)S(1)} %bitcast.8), channel_id=1, source_target_pairs={{0,24},{1,25},{2,26},{3,27},{4,28},{5,29},{6,30},{7,31},{8,16},{9,... | collective-permute-start | bytes 73736 | tf_op jit(solution)/shard_map/ppermute | solution.py:334
  7.9 3.4 %collective-permute-start.3 = (f32[3,8,768]{2,1,0:T(8,128)S(1)}, f32[3,8,768]{2,1,0:T(8,128)S(1)}, u32[]{:S(2)}, u32[]{:S(2)}) collective-permute-start(f32[3,8,768]{2,1,0:T(8,128)S(1)} %pad_maximum_fusion), channel_id=1, source_target_pairs={{0,2},{1,3},{2,0},{3,1},{4,6},{5,7},{6,4},{7,5},{8,10},{9,11},{10,... | collective-permute-start | bytes 221192 | tf_op jit(solution)/shard_map/ppermute | solution.py:334
  8.1 4.2 %collective-permute-start.4 = (f32[2,8,768]{2,1,0:T(8,128)S(1)}, f32[2,8,768]{2,1,0:T(8,128)S(1)}, u32[]{:S(2)}, u32[]{:S(2)}) collective-permute-start(f32[2,8,768]{2,1,0:T(8,128)S(1)} %get-tuple-element.66.blocks), channel_id=1, source_target_pairs={{0,4},{1,5},{2,6},{3,7},{4,0},{5,1},{6,2},{7,3},{8,12},{9,13},{10,... | collective-permute-start | bytes 147464 | tf_op jit(solution)/shard_map/ppermute | solution.py:334
  8.4 4.2 %collective-permute-start.5 = (f32[2,8,768]{2,1,0:T(8,128)S(1)}, f32[2,8,768]{2,1,0:T(8,128)S(1)}, u32[]{:S(2)}, u32[]{:S(2)}) collective-permute-start(f32[2,8,768]{2,1,0:T(8,128)S(1)} %get-tuple-element.66.blocks), channel_id=1, source_target_pairs={{0,6},{1,7},{2,4},{3,5},{4,2},{5,3},{6,0},{7,1},{8,14},{9,15},{10,... | collective-permute-start | bytes 147464 | tf_op jit(solution)/shard_map/ppermute | solution.py:334
  12.6 4.4 %collective-permute-start.6 = (f32[10,8,768]{2,1,0:T(8,128)S(1)}, f32[10,8,768]{2,1,0:T(8,128)S(1)}, u32[]{:S(2)}, u32[]{:S(2)}) collective-permute-start(f32[10,8,768]{2,1,0:T(8,128)S(1)} %slice_dynamic-update-slice_fusion.1.blocks), channel_id=1, source_target_pairs={{0,1},{1,0},{2,3},{3,2},{4,5},{5,4},{6,7},{7,6},{8,9},{9,8},{10,11... | collective-permute-start | bytes 737288 | tf_op jit(solution)/shard_map/ppermute | solution.py:334

commit v2 on v1

--- a/solution.py
+++ b/solution.py
@@ -178,7 +178,7 @@
     total_ref[...] = total
 
 
-def parts_kernel(group, parts, wanted, most, plan, blocks, factors_ref, before, *refs):
+def parts_kernel(group, parts, wanted, most, own_part, plan, blocks, factors_ref, before, *refs):
     low = group // 2
     total_ref = refs[-1]
     views = refs[len(refs) // 2 : -1]
@@ -204,7 +204,9 @@
     def branch(items):
         def run(total):
             if wake_own:
-                total = add_part(factors, blocks[blocks.shape[0] - 1], view_of(wake_own, 2), total)
+                other = lax.rem(lax.axis_index("band"), 2) - 1 if own_part == 3 else 0
+                block = blocks[blocks.shape[0] - 1 + other]
+                total = add_part(factors, block, view_of(wake_own, own_part), total)
             for item in range(items):
                 view = view_of(listed, targets[item])
                 total = add_part(factors, blocks[sources[item]], view, total)
@@ -217,24 +219,22 @@
 
 def first_parts_kernel(group, parts, most, plan, blocks, factors_ref, before, *refs):
     wanted = lambda same, part, bits, top: (None, None) if part else (same, top)
-    parts_kernel(group, parts, wanted, most, plan, blocks, factors_ref, before, *[None] * 3, *refs)
+    parts_kernel(group, parts, wanted, most, 0, plan, blocks, factors_ref, before, *[None] * 3, *refs)
 
 
 def last_kernel(group, parts, plan, blocks, extended_ref, factors_ref, before, *refs):
     own, earlier = refs[:3], refs[3:6]
     updated_ref, first_ref = refs[6:8]
-    newest, newest_own = refs[8:11], refs[11:14]
-    results, semaphores = refs[14:]
+    newest = refs[8:11]
+    results, semaphores = refs[11:]
     low = group // 2
     tops = group // low
     factors = factors_ref[...]
     used = used_wakes(plan)
     slots = [slot_of(plan, wake, group) for wake in range(LISTED)]
-    own_at = blocks.shape[0] - 2 + lax.rem(lax.axis_index("band"), 2)
 
     def first_branch(wakes):
         def run(total):
-            total = add_part(factors, blocks[own_at], view_of(newest_own, 0), total)
             for wake in range(wakes):
                 slot = slots[wake]
                 for part in range(parts):
@@ -268,7 +268,7 @@
     moved = point_factors(predicted)
 
     def second_branch(wakes):
-        views = [view_of(own, part) for part in range(own[0].shape[0])] + [view_of(newest_own, 0)]
+        views = [view_of(own, part) for part in range(own[0].shape[0])]
         for index in range(wakes * parts):
             views += [view_of(earlier, index), view_of(newest, index)]
 
@@ -347,7 +347,7 @@
             ((3, points), F32),
             ((2 * points, TERMS), BF16),
             ((2, LISTED), jnp.int32),
-            *buffers(3, seg_count),
+            *buffers(bands, seg_count),
             sums,
         ),
         in_specs=[VMEM] * 4,
@@ -356,9 +356,9 @@
         cost_estimate=cost(points, 2 * seg_count),
     )(upstream, upstream_mask, own, behind)
 
-    def add_parts(wanted, most, blocks, total, held):
+    def add_parts(wanted, most, own_part, blocks, total, held):
         *held, total = pl.pallas_call(
-            functools.partial(parts_kernel, group, parts, wanted, most),
+            functools.partial(parts_kernel, group, parts, wanted, most, own_part),
             out_shape=outs(*[(array.shape, array.dtype) for array in held], sums),
             in_specs=[VMEM] * (4 + len(held)),
             out_specs=(VMEM,) * (1 + len(held)),
@@ -391,16 +391,22 @@
         return ~same, (bits * parts + part) * tops + top
 
     with_own, total = lax.optimization_barrier((with_own, total))
+    early = flipped(jnp.concatenate([own, with_own[tops:]]), 0, 1)
     held, total = add_parts(
-        brought_across, some * (parts - 1), with_own, total, [*listed, *wake_own]
+        brought_across, some * (parts - 1), 2, with_own, total, [*listed, *wake_own]
+    )
+    *far, early, total = lax.optimization_barrier((*far, early, total))
+    far = jnp.concatenate([near, with_own[:tops], *far])
+    last = flipped(far, 0, 1)
+    held, total = add_parts(
+        brought_along,
+        min(LISTED, group - tops) * parts,
+        3,
+        jnp.concatenate([far, early]),
+        total,
+        held,
     )
     listed, wake_own = held[:3], held[3:]
-    *far, total = lax.optimization_barrier((*far, total))
-    far = jnp.concatenate([near, with_own[:tops], *far, own, with_own[tops:]])
-    last = flipped(far, 0, 1)
-    listed, total = add_parts(
-        brought_along, min(LISTED, group - tops) * parts, far, total, listed
-    )
 
     out = ((3, 1, count), F32)
     updated, first = pl.pallas_call(
@@ -410,7 +416,6 @@
         out_specs=(ANY,) * 2,
         scratch_shapes=[
             *[pltpu.VMEM(shape, dtype) for shape, dtype in buffers(LISTED * parts, seg_count)],
-            *[pltpu.VMEM(shape, dtype) for shape, dtype in buffers(1, seg_count)],
             pltpu.VMEM((2, 3, count), F32),
             pltpu.SemaphoreType.DMA((2, 3)),
         ],

time: 25 us -> 25.1 us (level)
    pallas_call x2, Pallas kernels: 2.51 us -> 2.81 us  [add_parts(): pl.pallas_call(functools.partial(parts_kernel, group, parts, wanted, most...]
    ppermute x7 -> x8, waiting for transfers between devices: 1.62 us -> 1.45 us  [permuted(): return lax.ppermute(blocks, ('row', 'band'), route)]
    ppermute x7 -> x8, starting transfers between devices: 9.64 us -> 9.77 us  [permuted(): return lax.ppermute(blocks, ('row', 'band'), route)]
  transfers between devices with their start and end apart: 7 -> 8, of which waited for: 3 -> 2; matrix products, arithmetic and copies ran while one was open for 0% -> 0% of each run, Pallas kernels for 17% -> 18%
where the time goes in v2:
time: 25.1 us
  Pallas kernels  12.9 us (51%)
  starting transfers between devices  9.77 us (39%)
  waiting for transfers between devices  1.45 us (6%)
  between operations  0.92 us (4%)
    ppermute x8, starting transfers between devices, permuted(): return lax.ppermute(blocks, ('row', 'band'), route)  9.77 us
    pallas_call x1, Pallas kernels, local(): pl.pallas_call(functools.partial(last_kernel, group, parts), out_shape=ou...  7.6 us
    pallas_call x2, Pallas kernels, add_parts(): pl.pallas_call(functools.partial(parts_kernel, group, parts, wanted, most...  2.81 us
    ppermute x8, waiting for transfers between devices, permuted(): return lax.ppermute(blocks, ('row', 'band'), route)  1.45 us
    pallas_call x1, Pallas kernels, local(): pl.pallas_call(functools.partial(own_kernel, count), out_shape=outs(((3,...  1 us
    pallas_call x1, Pallas kernels, local(): pl.pallas_call(pack_kernel, out_shape=pltpu.VMEM((8, seg_count), F32), in...  0.79 us
    pallas_call x1, Pallas kernels, local(): pl.pallas_call(functools.partial(first_parts_kernel, group, parts, some),...  0.68 us
  transfers between devices with their start and end apart: 8, of which 2 were waited for; matrix products, arithmetic and copies ran while one was open for 0% of the time, Pallas kernels for 18%

profile of v2, /device:TPU:29, one launch (start us, length us, event | category | flops | bytes accessed | tf_op | source)
XLA Modules:
  0.0 25.1 jit_solution(8434427883924708868)
XLA Ops:
  0.6 0.8 %shard_map.68 = f32[8,768]{1,0:T(8,128)S(1)} custom-call(f32[3,1,128]{2,1,0:T(1,128)} %bitcast.12, f32[6,1,768]{2,1,0:T(1,128)} %bitcast.11, f32[1,768]{1,0:T(1,128)} %circulation.1), custom_call_target="tpu_custom_call" | custom-call | tf_op jit(solution)/shard_map/pallas_call | solution.py:321
  1.4 0.0 copy-start
  1.4 0.0 copy-start.1
  1.5 1.8 %collective-permute-start = (f32[1,8,768]{2,1,0:T(8,128)S(1)}, f32[1,8,768]{2,1,0:T(8,128)S(1)}, u32[]{:S(2)}, u32[]{:S(2)}) collective-permute-start(f32[1,8,768]{2,1,0:T(8,128)S(1)} %bitcast.5), channel_id=1, source_target_pairs={{0,1},{1,2},{2,3},{3,0},{4,5},{5,6},{6,7},{7,4},{8,9},{9,10},{10,1... | collective-permute-start | bytes 73736 | tf_op jit(solution)/shard_map/ppermute | solution.py:334
  3.3 0.1 collective-permute-start.1
  3.3 2.2 %collective-permute-start.2 = (f32[1,8,768]{2,1,0:T(8,128)S(1)}, f32[1,8,768]{2,1,0:T(8,128)S(1)}, u32[]{:S(2)}, u32[]{:S(2)}) collective-permute-start(f32[1,8,768]{2,1,0:T(8,128)S(1)} %bitcast.7), channel_id=1, source_target_pairs={{0,24},{1,25},{2,26},{3,27},{4,28},{5,29},{6,30},{7,31},{8,16},{9,... | collective-permute-start | bytes 73736 | tf_op jit(solution)/shard_map/ppermute | solution.py:334
  5.5 0.0 collective-permute-done.behind
  5.5 0.0 copy-done
  5.5 0.0 copy-done.1
  5.5 1.0 %shard_map.69 = (f32[3,144]{1,0:T(4,128)S(1)}, bf16[288,96]{1,0:T(8,128)(2,1)S(1)}, s32[2,3]{1,0:T(2,128)S(1)}, bf16[4,96,768]{2,1,0:T(8,128)(2,1)S(1)}, bf16[4,...) custom-call(s32[1,3]{1,0:T(1,128)S(1)} %copy-done, s32[1,3]{1,0:T(1,128)S(1)} %copy-done.1, ...), custom_call_target="tpu_custom_call" | custom-call | flops 110592000 | bytes 614400 | tf_op jit(solution)/shard_map/pallas_call | solution.py:344
  6.5 1.0 %collective-permute-done.1 = f32[1,8,768]{2,1,0:T(8,128)S(1)} collective-permute-done((f32[1,8,768]{2,1,0:T(8,128)S(1)}, f32[1,8,768]{2,1,0:T(8,128)S(1)}, u32[]{:S(2)}, u32[]{:S(2)}) %collective-permute-start.1) | collective-permute-done | bytes 24608 | tf_op jit(solution)/shard_map/ppermute | solution.py:334
  7.5 0.4 %collective-permute-done.2 = f32[1,8,768]{2,1,0:T(8,128)S(1)} collective-permute-done((f32[1,8,768]{2,1,0:T(8,128)S(1)}, f32[1,8,768]{2,1,0:T(8,128)S(1)}, u32[]{:S(2)}, u32[]{:S(2)}) %collective-permute-start.2) | collective-permute-done | bytes 24608 | tf_op jit(solution)/shard_map/ppermute | solution.py:334
  7.9 0.2 collective-permute-start.3
  8.2 0.2 collective-permute-start.4
  8.4 2.3 %collective-permute-start.5 = (f32[2,8,768]{2,1,0:T(8,128)S(1)}, f32[2,8,768]{2,1,0:T(8,128)S(1)}, u32[]{:S(2)}, u32[]{:S(2)}) collective-permute-start(f32[2,8,768]{2,1,0:T(8,128)S(1)} %get-tuple-element.82.blocks), channel_id=1, source_target_pairs={{0,6},{1,7},{2,4},{3,5},{4,2},{5,3},{6,0},{7,1},{8,14},{9,15},{10,... | collective-permute-start | bytes 147464 | tf_op jit(solution)/shard_map/ppermute | solution.py:334
  10.6 0.7 %shard_map.70 = (bf16[6,96,768]{2,1,0:T(8,128)(2,1)S(1)}, bf16[6,32,768]{2,1,0:T(8,128)(2,1)S(1)}, f32[6,1,768]{2,1,0:T(1,128)S(1)}, f32[32,144]{1,0:T(8,128)S(1)}) custom-call(s32[2,3]{1,0:T(2,128)S(1)} %get-tuple-element.38.plan, f32[2,8,768]{2,1,0:T(8,128)S(1)} %get-tuple-element.82.blocks, bf16[288,96]{1,0:T(8,128)(2,1)S(1)} %get-tuple-element.42.factors_ref, ...), custom_call_target="tpu_custom_call" | custom-call | flops 165888000 | bytes 921600 | tf_op jit(solution)/shard_map/pallas_call | solution.py:378
  11.3 0.0 collective-permute-done.3.blocks
  11.4 1.8 %collective-permute-start.6 = (f32[2,8,768]{2,1,0:T(8,128)S(1)}, f32[2,8,768]{2,1,0:T(8,128)S(1)}, u32[]{:S(2)}, u32[]{:S(2)}) collective-permute-start(f32[2,8,768]{2,1,0:T(8,128)S(1)} %pad_maximum_fusion.1), channel_id=1, source_target_pairs={{0,1},{1,0},{2,3},{3,2},{4,5},{5,4},{6,7},{7,6},{8,9},{9,8},{10,11... | collective-permute-start | bytes 147464 | tf_op jit(solution)/shard_map/ppermute | solution.py:334
  13.2 1.0 %shard_map.71 = (bf16[6,96,768]{2,1,0:T(8,128)(2,1)S(1)}, bf16[6,32,768]{2,1,0:T(8,128)(2,1)S(1)}, f32[6,1,768]{2,1,0:T(1,128)S(1)}, bf16[4,96,768]{2,1,0:T(8,12...) custom-call(s32[2,3]{1,0:T(2,128)S(1)} %get-tuple-element.38.plan, ...), custom_call_target="tpu_custom_call", output_to_operand_aliasing={{0}: (4, {}), {1}: (5, {}), {2}: (6, {}), {3}: (7, {}), {4}... | custom-call | flops 165888000 | bytes 921600 | tf_op jit(solution)/shard_map/pallas_call | solution.py:360
  14.2 0.0 collective-permute-done.4
  14.2 0.0 collective-permute-done.5
  14.2 0.0 collective-permute-done.6
  14.3 1.1 %collective-permute-start.7 = (f32[8,8,768]{2,1,0:T(8,128)S(1)}, f32[8,8,768]{2,1,0:T(8,128)S(1)}, u32[]{:S(2)}, u32[]{:S(2)}) collective-permute-start(f32[8,8,768]{2,1,0:T(8,128)S(1)} %get-tuple-element.77), channel_id=1, source_target_pairs={{0,1},{1,0},{2,3},{3,2},{4,5},{5,4},{6,7},{7,6},{8,9},{9,8},{10,11... | collective-permute-start | bytes 589832 | tf_op jit(solution)/shard_map/ppermute | solution.py:334
  15.4 1.9 %shard_map.72 = (bf16[6,96,768]{2,1,0:T(8,128)(2,1)S(1)}, bf16[6,32,768]{2,1,0:T(8,128)(2,1)S(1)}, f32[6,1,768]{2,1,0:T(1,128)S(1)}, bf16[4,96,768]{2,1,0:T(8,12...) custom-call(s32[2,3]{1,0:T(2,128)S(1)} %get-tuple-element.38.plan, ...), custom_call_target="tpu_custom_call", output_to_operand_aliasing={{0}: (4, {}), {1}: (5, {}), {2}: (6, {}), {3}: (7, {}), {4}... | custom-call | flops 165888000 | bytes 921600 | tf_op jit(solution)/shard_map/pallas_call | solution.py:360
  17.3 0.0 collective-permute-done.7.blocks
  17.3 7.6 %shard_map.73 = (f32[3,1,128]{2,1,0:T(1,128)}, f32[3,1,128]{2,1,0:T(1,128)}) custom-call(s32[2,3]{1,0:T(2,128)S(1)} %get-tuple-element.38.plan, f32[8,8,768]{2,1,0:T(8,128)S(1)} %collective-permute-done.7.blocks, f32[3,144]{1,0:T(4,128)S(1)} %get-tuple-element.56.extended_ref, bf16[288,96]{1,0:T(8,128)(2,1)S(1)} %get-tuple-element.42.factors_ref, ...), custom_call_target="tpu_custom_call" | custom-call | flops 884736000 | bytes 4915200 | tf_op jit(solution)/shard_map/pallas_call | solution.py:412
  (9 shorter events, 0.1 us)
Async XLA Ops:
  1.4 4.1 %copy-start = (s32[1,3]{1,0:T(1,128)S(1)}, s32[1,3]{1,0:T(1,128)}, u32[]{:S(2)}) copy-start(s32[1,3]{1,0:T(1,128)} %upstream.1) | copy-start | bytes 40
  1.4 4.1 %copy-start.1 = (s32[1,3]{1,0:T(1,128)S(1)}, s32[1,3]{1,0:T(1,128)}, u32[]{:S(2)}) copy-start(s32[1,3]{1,0:T(1,128)} %mask.1) | copy-start | bytes 40
  1.5 4.1 %collective-permute-start = (f32[1,8,768]{2,1,0:T(8,128)S(1)}, f32[1,8,768]{2,1,0:T(8,128)S(1)}, u32[]{:S(2)}, u32[]{:S(2)}) collective-permute-start(f32[1,8,768]{2,1,0:T(8,128)S(1)} %bitcast.5), channel_id=1, source_target_pairs={{0,1},{1,2},{2,3},{3,0},{4,5},{5,6},{6,7},{7,4},{8,9},{9,10},{10,1... | collective-permute-start | bytes 73736 | tf_op jit(solution)/shard_map/ppermute | solution.py:334
  3.3 4.3 %collective-permute-start.1 = (f32[1,8,768]{2,1,0:T(8,128)S(1)}, f32[1,8,768]{2,1,0:T(8,128)S(1)}, u32[]{:S(2)}, u32[]{:S(2)}) collective-permute-start(f32[1,8,768]{2,1,0:T(8,128)S(1)} %bitcast.6), channel_id=1, source_target_pairs={{0,16},{1,17},{2,18},{3,19},{4,20},{5,21},{6,22},{7,23},{8,24},{9,... | collective-permute-start | bytes 73736 | tf_op jit(solution)/shard_map/ppermute | solution.py:334
  3.3 4.6 %collective-permute-start.2 = (f32[1,8,768]{2,1,0:T(8,128)S(1)}, f32[1,8,768]{2,1,0:T(8,128)S(1)}, u32[]{:S(2)}, u32[]{:S(2)}) collective-permute-start(f32[1,8,768]{2,1,0:T(8,128)S(1)} %bitcast.7), channel_id=1, source_target_pairs={{0,24},{1,25},{2,26},{3,27},{4,28},{5,29},{6,30},{7,31},{8,16},{9,... | collective-permute-start | bytes 73736 | tf_op jit(solution)/shard_map/ppermute | solution.py:334
  7.9 3.4 %collective-permute-start.3 = (f32[3,8,768]{2,1,0:T(8,128)S(1)}, f32[3,8,768]{2,1,0:T(8,128)S(1)}, u32[]{:S(2)}, u32[]{:S(2)}) collective-permute-start(f32[3,8,768]{2,1,0:T(8,128)S(1)} %pad_maximum_fusion), channel_id=1, source_target_pairs={{0,2},{1,3},{2,0},{3,1},{4,6},{5,7},{6,4},{7,5},{8,10},{9,11},{10,... | collective-permute-start | bytes 221192 | tf_op jit(solution)/shard_map/ppermute | solution.py:334
  8.2 6.1 %collective-permute-start.4 = (f32[2,8,768]{2,1,0:T(8,128)S(1)}, f32[2,8,768]{2,1,0:T(8,128)S(1)}, u32[]{:S(2)}, u32[]{:S(2)}) collective-permute-start(f32[2,8,768]{2,1,0:T(8,128)S(1)} %get-tuple-element.82.blocks), channel_id=1, source_target_pairs={{0,4},{1,5},{2,6},{3,7},{4,0},{5,1},{6,2},{7,3},{8,12},{9,13},{10,... | collective-permute-start | bytes 147464 | tf_op jit(solution)/shard_map/ppermute | solution.py:334
  8.4 5.9 %collective-permute-start.5 = (f32[2,8,768]{2,1,0:T(8,128)S(1)}, f32[2,8,768]{2,1,0:T(8,128)S(1)}, u32[]{:S(2)}, u32[]{:S(2)}) collective-permute-start(f32[2,8,768]{2,1,0:T(8,128)S(1)} %get-tuple-element.82.blocks), channel_id=1, source_target_pairs={{0,6},{1,7},{2,4},{3,5},{4,2},{5,3},{6,0},{7,1},{8,14},{9,15},{10,... | collective-permute-start | bytes 147464 | tf_op jit(solution)/shard_map/ppermute | solution.py:334
  11.4 2.9 %collective-permute-start.6 = (f32[2,8,768]{2,1,0:T(8,128)S(1)}, f32[2,8,768]{2,1,0:T(8,128)S(1)}, u32[]{:S(2)}, u32[]{:S(2)}) collective-permute-start(f32[2,8,768]{2,1,0:T(8,128)S(1)} %pad_maximum_fusion.1), channel_id=1, source_target_pairs={{0,1},{1,0},{2,3},{3,2},{4,5},{5,4},{6,7},{7,6},{8,9},{9,8},{10,11... | collective-permute-start | bytes 147464 | tf_op jit(solution)/shard_map/ppermute | solution.py:334
  14.3 3.0 %collective-permute-start.7 = (f32[8,8,768]{2,1,0:T(8,128)S(1)}, f32[8,8,768]{2,1,0:T(8,128)S(1)}, u32[]{:S(2)}, u32[]{:S(2)}) collective-permute-start(f32[8,8,768]{2,1,0:T(8,128)S(1)} %get-tuple-element.77), channel_id=1, source_target_pairs={{0,1},{1,0},{2,3},{3,2},{4,5},{5,4},{6,7},{7,6},{8,9},{9,8},{10,11... | collective-permute-start | bytes 589832 | tf_op jit(solution)/shard_map/ppermute | solution.py:334
